TPU v7x, 32 devices: a whole 2x2x4 slice. The times are simulated.
32 devices in a mesh: groups: 2 (over y), ctx: 4 (over z), dp: 2 (over x), mp: 2 (over core).
Axes of the slice: x: 2, y: 2, z: 4, core: 2. Of those that a mesh axis runs over, the one named last changes fastest.
Arguments:
- byte_ids: int32 [4, 1024], P(('groups', 'dp'), 'ctx'), parts along dimension 0, may hold values from 0 to 255
- lengths: int32 [4], P(('groups', 'dp')), parts along dimension 0, may hold values from 128 to 1024, as said below
- hidden: bfloat16 [4, 256, 768], P(('groups', 'dp'), 'ctx'), parts along dimension 0
- w_qkv: bfloat16 [768, 3, 768], P(None, None, 'mp'), may hold values from -0.21875 to 0.21875
- w_out: bfloat16 [768, 768], P('mp'), may hold values from -0.21875 to 0.21875
- w_up: bfloat16 [4, 768, 768], P(None, None, 'mp'), may hold values from -0.109375 to 0.109375
- w_head: bfloat16 [768, 256], P('mp'), may hold values from -0.21875 to 0.21875
Outputs:
- grad_hidden: bfloat16 [4, 256, 768], P(('groups', 'dp'), 'ctx'), parts along dimension 0
There are 2 independent parts, one for each index of `groups`. A program takes and returns all parts, laid end to end along the dimension named above; an argument that names none is the same for every part. Nothing has to cross between parts.
Inputs may be any that keep to these rules, and one draw needn't show every extreme that they name: `lengths`: each document's valid byte count; in every draw some document is full, with 1024 valid bytes.
All inputs are finite; a program needn't handle non-finite values.
Results may differ from a plain program's by a relative error of at most 0.025.
Values may be sent and summed in bfloat16 or wider, within the bound.
A program may use at most 64 MiB of HBM per device.

v0:
```python
import jax
import jax.numpy as jnp
from jax import lax
from jax.sharding import PartitionSpec as P

HEAD_DIM = 64


def with_halo(x, sides, width):
    for axis, dim in sides:
        devices, length = (lax.axis_size(axis), x.shape[dim])
        up = [(i, (i + 1) % devices) for i in range(devices - 1)]
        down = [(j, i) for i, j in up]
        last = lax.slice_in_dim(x, length - width, length, axis=dim)
        initial = lax.slice_in_dim(x, 0, width, axis=dim)
        before = lax.ppermute(last, axis, up)
        after = lax.ppermute(initial, axis, down)
        x = jnp.concatenate([before, x, after], axis=dim)
    return x


def pair_sum(values):
    return lax.psum(values, "mp")


def edges(values):
    return with_halo(values, (("ctx", 0),), 1)


def gelu_grad(pre_act, incoming):
    result, pullback = jax.vjp(jax.nn.gelu, pre_act)
    return pullback(incoming)[0]


def body(byte_ids, lengths, hidden, w_qkv, w_out, w_up, w_head):
    inputs = hidden[0]
    rows = inputs.shape[0]
    model_width = inputs.shape[1]
    split_width = w_qkv.shape[2]
    own_heads = split_width // HEAD_DIM
    scaling = HEAD_DIM ** (-0.5)
    length = lengths[0]
    my_first = lax.axis_index("ctx") * rows
    byte_rows = 4 * rows
    flat_qkv = w_qkv.reshape(model_width, 3 * split_width)
    projected = jnp.dot(inputs, flat_qkv, preferred_element_type=jnp.float32).astype(jnp.bfloat16)
    projected = projected.reshape(rows, 3, own_heads, HEAD_DIM)
    queries = projected[:, 0]
    key_rows = projected[:, 1]
    value_rows = projected[:, 2]

    def usable(first_row, count):
        return 4 * (first_row + jnp.arange(count, dtype=jnp.int32)) < length

    running = jnp.full((rows, own_heads), -1e30, jnp.float32)
    key_piece = lax.all_gather(key_rows, "ctx", axis=0, tiled=True)
    value_piece = lax.all_gather(value_rows, "ctx", axis=0, tiled=True)
    keep = usable(jnp.int32(0), key_piece.shape[0])[None, None, :]
    scores = (
        jnp.einsum("qhd,khd->qhk", queries, key_piece, preferred_element_type=jnp.float32) * scaling
    )
    newest = jnp.maximum(running, jnp.max(jnp.where(keep, scores, -1e30), axis=-1))
    weights = jnp.where(keep, jnp.exp(scores - newest[..., None]), 0.0)
    totals = jnp.sum(weights, axis=-1)
    weighted = jnp.einsum(
        "qhk,khd->qhd",
        weights.astype(jnp.bfloat16),
        value_piece,
        preferred_element_type=jnp.float32,
    )
    weighted, running, totals = (weighted, newest, totals)
    attn_heads = (weighted / totals[..., None]).astype(jnp.bfloat16)
    attn = attn_heads.reshape(rows, split_width)
    log_norm = running + jnp.log(totals)
    context = (
        inputs.astype(jnp.float32)
        + pair_sum(jnp.dot(attn, w_out, preferred_element_type=jnp.float32))
    ).astype(jnp.bfloat16)
    extended = edges(context)
    tap_outputs = [
        jnp.dot(extended, w_up[tap], preferred_element_type=jnp.float32) for tap in range(4)
    ]
    phases = []
    for phase in range(4):
        phase_sum = jnp.zeros((rows, split_width), jnp.float32)
        for tap in range(4):
            shifted = 1 + (phase + tap - 1) // 4
            phase_sum = phase_sum + tap_outputs[tap][shifted : shifted + rows]
        phases.append(phase_sum)
    pre_act = jnp.stack(phases, axis=1).reshape(byte_rows, split_width)
    activated = jax.nn.gelu(pre_act).astype(jnp.bfloat16)
    logits = pair_sum(jnp.dot(activated, w_head, preferred_element_type=jnp.float32))
    byte_first = lax.axis_index("ctx") * byte_rows
    byte_mask = byte_first + jnp.arange(byte_rows, dtype=jnp.int32) < length
    inverse = 1.0 / length.astype(jnp.float32)
    softmaxed = jax.nn.softmax(logits, axis=-1)
    onehot = (byte_ids[0][:, None] == jnp.arange(logits.shape[1], dtype=jnp.int32)[None, :]).astype(
        jnp.float32
    )
    logit_grad = ((softmaxed - onehot) * jnp.where(byte_mask, inverse, 0.0)[:, None]).astype(
        jnp.bfloat16
    )
    act_grad = jnp.dot(logit_grad, w_head.T, preferred_element_type=jnp.float32)
    pre_grad = gelu_grad(pre_act, act_grad).astype(jnp.bfloat16)
    grad_ext = edges(pre_grad.reshape(rows, 4 * split_width)).reshape(byte_rows + 8, split_width)
    partial_grad = jnp.zeros((rows, model_width), jnp.float32)
    for offset in range(4):
        window = grad_ext[5 - offset : 5 - offset + byte_rows].astype(jnp.float32)
        tap_sum = jnp.sum(window.reshape(rows, 4, split_width), axis=1).astype(jnp.bfloat16)
        partial_grad = partial_grad + jnp.dot(
            tap_sum, w_up[offset].T, preferred_element_type=jnp.float32
        )
    context_grad = pair_sum(partial_grad)
    attn_grad = jnp.dot(
        context_grad.astype(jnp.bfloat16), w_out.T, preferred_element_type=jnp.float32
    ).astype(jnp.bfloat16)
    attn_grad = attn_grad.reshape(rows, own_heads, HEAD_DIM)
    row_dots = jnp.sum(attn_grad.astype(jnp.float32) * attn_heads.astype(jnp.float32), axis=-1)
    key_piece = lax.all_gather(key_rows, "ctx", axis=0, tiled=True)
    value_piece = lax.all_gather(value_rows, "ctx", axis=0, tiled=True)
    keep = usable(jnp.int32(0), key_piece.shape[0])[None, None, :]
    scores = (
        jnp.einsum("qhd,khd->qhk", queries, key_piece, preferred_element_type=jnp.float32) * scaling
    )
    probs = jnp.where(keep, jnp.exp(scores - log_norm[..., None]), 0.0)
    product = jnp.einsum("qhd,khd->qhk", attn_grad, value_piece, preferred_element_type=jnp.float32)
    score_grad = (probs * (product - row_dots[..., None])).astype(jnp.bfloat16)
    query_sum = jnp.einsum(
        "qhk,khd->qhd", score_grad, key_piece, preferred_element_type=jnp.float32
    )
    query_grad = (query_sum * scaling).astype(jnp.bfloat16)
    key_keep = usable(my_first, rows)[None, None, :]
    norm_all, dots_all = (
        lax.all_gather(log_norm, "ctx", axis=0, tiled=True),
        lax.all_gather(row_dots, "ctx", axis=0, tiled=True),
    )
    query_piece = lax.all_gather(queries, "ctx", axis=0, tiled=True)
    outgrad_piece = lax.all_gather(attn_grad, "ctx", axis=0, tiled=True)
    count = query_piece.shape[0]
    scores = (
        jnp.einsum("qhd,khd->qhk", query_piece, key_rows, preferred_element_type=jnp.float32)
        * scaling
    )
    probs = jnp.where(key_keep, jnp.exp(scores - norm_all[..., None]), 0.0)
    product = jnp.einsum(
        "qhd,khd->qhk", outgrad_piece, value_rows, preferred_element_type=jnp.float32
    )
    score_grad = (probs * (product - dots_all[..., None])).astype(jnp.bfloat16)
    key_sum = jnp.einsum(
        "qhk,qhd->khd", score_grad, query_piece, preferred_element_type=jnp.float32
    )
    value_sum = jnp.einsum(
        "qhk,qhd->khd",
        probs.astype(jnp.bfloat16),
        outgrad_piece,
        preferred_element_type=jnp.float32,
    )
    key_sum, value_sum = (key_sum, value_sum)
    key_grad = (key_sum * scaling).astype(jnp.bfloat16)
    value_grad = value_sum.astype(jnp.bfloat16)
    stacked = jnp.stack([query_grad, key_grad, value_grad], axis=1).reshape(rows, 3 * split_width)
    back_proj = pair_sum(jnp.dot(stacked, flat_qkv.T, preferred_element_type=jnp.float32))
    input_grad = (context_grad + back_proj).astype(jnp.bfloat16)
    return input_grad[None]


def solution(mesh):
    placed = (
        P(("groups", "dp"), "ctx"),
        P(("groups", "dp")),
        P(("groups", "dp"), "ctx", None),
        P(None, None, "mp"),
        P("mp", None),
        P(None, None, "mp"),
        P("mp", None),
    )
    return jax.shard_map(
        body,
        mesh=mesh,
        in_specs=placed,
        out_specs=P(("groups", "dp"), "ctx", None),
        check_vma=False,
    )
```

profile of v0, /device:TPU:0, one launch (start us, length us, event | category | flops | bytes accessed | tf_op | source)
XLA Modules:
  0.0 255.1 jit_solution(12642925866357019696)
XLA Ops:
  7.3 2.6 %copy.24 = bf16[768,3,384]{0,2,1:T(8,128)(2,1)S(1)} copy(bf16[768,3,384]{2,0,1:T(8,128)(2,1)} %param.10) | data formatting | bytes 3538944 | tf_op args[3]
  12.2 17.3 %all-gather.1 = bf16[256,1,6,64]{3,2,1,0:T(8,128)(2,1)S(1)} all-gather(bf16[64,1,6,64]{3,2,1,0:T(8,128)(2,1)S(1)} %get-tuple-element.11), channel_id=3, replica_groups=mesh['groups'=2,'ctx'=4,'dp'=2,'mp'=2] {'ctx'}, dimensions={0}, use_global_device_ids=true | all-gather | bytes 245760 | tf_op jit(solution)/shard_map/all_gather | solution.py:56
  32.7 16.3 %all-gather = bf16[256,1,6,64]{3,2,1,0:T(8,128)(2,1)S(1)} all-gather(bf16[64,1,6,64]{3,2,1,0:T(8,128)(2,1)S(1)} %get-tuple-element.9), channel_id=2, replica_groups=mesh['groups'=2,'ctx'=4,'dp'=2,'mp'=2] {'ctx'}, dimensions={0}, use_global_device_ids=true | all-gather | bytes 245760 | tf_op jit(solution)/shard_map/all_gather | solution.py:57
  52.5 18.5 %all-reduce.5.cloned.1.call-done = f32[64,768]{1,0:T(8,128)} async-done(((f32[64,768]{1,0:T(8,128)}), f32[64,768]{1,0:T(8,128)}) %all-reduce.5.cloned.1.call-update) | async-done | bytes 196624 | tf_op jit(solution)/shard_map/psum | solution.py:23
  72.0 3.6 %collective-permute-start = (bf16[1,768]{1,0:T(2,128)(2,1)S(1)}, bf16[1,768]{1,0:T(2,128)(2,1)S(1)}, u32[]{:S(2)}, u32[]{:S(2)}) collective-permute-start(bf16[1,768]{1,0:T(2,128)(2,1)S(1)} %get-tuple-element.17), channel_id=1, source_target_pairs={{0,4},{4,8},{8,12},{1,5},{5,9},{9,13},{2,6},{6,10},{10,14},{3,7},{... | collective-permute-start | bytes 4616 | tf_op jit(solution)/shard_map/ppermute | solution.py:16
  77.0 4.2 %collective-permute-done.1 = bf16[1,768]{1,0:T(2,128)(2,1)S(1)} collective-permute-done((bf16[1,768]{1,0:T(2,128)(2,1)S(1)}, bf16[1,768]{1,0:T(2,128)(2,1)S(1)}, u32[]{:S(2)}, u32[]{:S(2)}) %collective-permute-start.1) | collective-permute-done | bytes 1568 | tf_op jit(solution)/shard_map/ppermute | solution.py:17
  87.6 2.0 fusion.67
  90.2 17.8 %all-reduce.7.cloned.1.call-done = f32[256,256]{1,0:T(8,128)} async-done(((f32[256,256]{1,0:T(8,128)}), f32[256,256]{1,0:T(8,128)}) %all-reduce.7.cloned.1.call-update) | async-done | bytes 262160 | tf_op jit(solution)/shard_map/psum | solution.py:23
  110.2 1.6 fusion.45
  111.9 4.2 %collective-permute-start.2 = (bf16[1,1536]{1,0:T(2,128)(2,1)S(1)}, bf16[1,1536]{1,0:T(2,128)(2,1)}, u32[]{:S(2)}, u32[]{:S(2)}) collective-permute-start(bf16[1,1536]{1,0:T(2,128)(2,1)S(1)} %bitcast.170), channel_id=1, source_target_pairs={{0,4},{4,8},{8,12},{1,5},{5,9},{9,13},{2,6},{6,10},{10,14},{3,7},{... | collective-permute-start | bytes 9224 | tf_op jit(solution)/shard_map/ppermute | solution.py:16
  118.0 15.7 %all-gather.2 = bf16[256,1,6,64]{3,0,2,1:T(8,128)(2,1)S(1)} all-gather(bf16[64,1,6,64]{3,0,2,1:T(8,128)(2,1)S(1)} %copy.46), channel_id=4, replica_groups=mesh['groups'=2,'ctx'=4,'dp'=2,'mp'=2] {'ctx'}, dimensions={0}, use_global_device_ids=true | all-gather | bytes 245760 | tf_op jit(solution)/shard_map/all_gather | solution.py:137
  133.7 13.4 %all-gather.3 = f32[4,64,6]{1,2,0:T(8,128)S(1)} all-gather(f32[1,64,6]{1,2,0:T(8,128)S(1)} %bitcast.168), channel_id=1, replica_groups=mesh['groups'=2,'ctx'=4,'dp'=2,'mp'=2] {'ctx'}, dimensions={0}, use_global_device_ids=true | all-gather | bytes 7680 | tf_op jit(solution)/shard_map/all_gather | solution.py:134
  148.1 1.8 reduce_sum.69
  155.1 2.1 fusion.27
  162.2 2.1 convolution_add_fusion
  165.5 18.4 %all-reduce.9.cloned.1.call-done = f32[64,768]{1,0:T(8,128)} async-done(((f32[64,768]{1,0:T(8,128)}), f32[64,768]{1,0:T(8,128)}) %all-reduce.9.cloned.1.call-update) | async-done | bytes 196624 | tf_op jit(solution)/shard_map/psum | solution.py:23
  183.9 1.9 convolution_convert_fusion.2
  185.7 1.5 copy.33
  188.2 1.7 copy.37
  189.9 2.1 fusion.16
  192.0 13.4 %all-gather.4 = f32[4,64,6]{1,2,0:T(8,128)S(1)} all-gather(f32[1,64,6]{1,2,0:T(8,128)S(1)} %bitcast.169), channel_id=1, replica_groups=mesh['groups'=2,'ctx'=4,'dp'=2,'mp'=2] {'ctx'}, dimensions={0}, use_global_device_ids=true | all-gather | bytes 7680 | tf_op jit(solution)/shard_map/all_gather | solution.py:135
  205.5 17.8 %all_gather.24 = bf16[256,6,64]{2,1,0:T(8,128)(2,1)} all-gather(bf16[64,6,64]{2,1,0:T(8,128)(2,1)} %copy.37), channel_id=1, replica_groups=mesh['groups'=2,'ctx'=4,'dp'=2,'mp'=2] {'ctx'}, dimensions={0}, use_global_device_ids=true | all-gather | bytes 245760 | tf_op jit(solution)/shard_map/all_gather | solution.py:138
  228.9 18.0 %all-reduce.11.cloned.1.call-done = f32[64,768]{1,0:T(8,128)} async-done(((f32[64,768]{1,0:T(8,128)}), f32[64,768]{1,0:T(8,128)}) %all-reduce.11.cloned.1.call-update) | async-done | bytes 196624 | tf_op jit(solution)/shard_map/psum | solution.py:23
  246.9 1.7 fusion.75
  (86 shorter events, 41.1 us)
Async XLA Ops:
  6.5 44.9 %copy-start = (bf16[384,768]{1,0:T(8,128)(2,1)S(1)}, bf16[384,768]{1,0:T(8,128)(2,1)}, u32[]{:S(2)}) copy-start(bf16[384,768]{1,0:T(8,128)(2,1)} %param.11) | copy-start | bytes 1769476
  6.5 3.4 %copy-start.3 = (bf16[1,64,768]{2,1,0:T(8,128)(2,1)S(1)}, bf16[1,64,768]{2,1,0:T(8,128)(2,1)}, u32[]{:S(2)}) copy-start(bf16[1,64,768]{2,1,0:T(8,128)(2,1)} %param.9) | copy-start | bytes 294916
  6.5 64.5 %all-reduce.5.cloned.1.call-start = ((), (), s32[]{:S(2)}) async-start(), calls=%async_computation | async-start | bytes 393216 | tf_op jit(solution)/shard_map/psum | solution.py:23
  7.3 42.9 %copy-start.8 = (pred[256]{0:T(512)(128)(4,1)}, pred[256]{0:T(512)(128)(4,1)S(1)}, u32[]{:S(2)}) copy-start(pred[256]{0:T(512)(128)(4,1)S(1)} %multiply_compare_fusion) | copy-start | bytes 772
  11.6 0.7 copy-start.2
  11.6 39.8 %copy-start.1 = (bf16[64,1,6,64]{3,2,1,0:T(8,128)(2,1)}, bf16[64,1,6,64]{3,2,1,0:T(8,128)(2,1)S(1)}, u32[]{:S(2)}) copy-start(bf16[64,1,6,64]{3,2,1,0:T(8,128)(2,1)S(1)} %get-tuple-element.9) | copy-start | bytes 147460
  49.9 21.1 %copy-start.4 = (bf16[1,64,768]{2,1,0:T(8,128)(2,1)S(1)}, bf16[1,64,768]{2,1,0:T(8,128)(2,1)}, u32[]{:S(2)}) copy-start(bf16[1,64,768]{2,1,0:T(8,128)(2,1)} %param.9) | copy-start | bytes 294916
  51.4 35.0 %copy-start.5 = (bf16[64,6,64]{0,2,1:T(8,128)(2,1)}, bf16[64,6,64]{0,2,1:T(8,128)(2,1)S(1)}, u32[]{:S(2)}) copy-start(bf16[64,6,64]{0,2,1:T(8,128)(2,1)S(1)} %fusion.12) | copy-start | bytes 147460
  52.4 55.6 %all-reduce.7.cloned.1.call-start = ((), (), s32[]{:S(2)}) async-start(), calls=%async_computation.1 | async-start | bytes 524288 | tf_op jit(solution)/shard_map/psum | solution.py:23
  72.0 5.0 %collective-permute-start = (bf16[1,768]{1,0:T(2,128)(2,1)S(1)}, bf16[1,768]{1,0:T(2,128)(2,1)S(1)}, u32[]{:S(2)}, u32[]{:S(2)}) collective-permute-start(bf16[1,768]{1,0:T(2,128)(2,1)S(1)} %get-tuple-element.17), channel_id=1, source_target_pairs={{0,4},{4,8},{8,12},{1,5},{5,9},{9,13},{2,6},{6,10},{10,14},{3,7},{... | collective-permute-start | bytes 4616 | tf_op jit(solution)/shard_map/ppermute | solution.py:16
  75.6 5.5 %collective-permute-start.1 = (bf16[1,768]{1,0:T(2,128)(2,1)S(1)}, bf16[1,768]{1,0:T(2,128)(2,1)S(1)}, u32[]{:S(2)}, u32[]{:S(2)}) collective-permute-start(bf16[1,768]{1,0:T(2,128)(2,1)S(1)} %get-tuple-element.18), channel_id=1, source_target_pairs={{4,0},{8,4},{12,8},{5,1},{9,5},{13,9},{6,2},{10,6},{14,10},{7,3},{... | collective-permute-start | bytes 4616 | tf_op jit(solution)/shard_map/ppermute | solution.py:17
  86.4 23.8 %copy-start.9 = (s32[1,256]{1,0:T(1,128)S(1)}, s32[1,256]{1,0:T(1,128)}, u32[]{:S(2)}) copy-start(s32[1,256]{1,0:T(1,128)} %param.7) | copy-start | bytes 3076
  89.6 94.2 %all-reduce.9.cloned.1.call-start = ((), (), s32[]{:S(2)}) async-start(), calls=%async_computation.2 | async-start | bytes 393216 | tf_op jit(solution)/shard_map/psum | solution.py:23
  90.2 43.5 %copy-start.6 = (f32[64,6]{0,1:T(8,128)}, f32[64,6]{0,1:T(8,128)S(1)}, u32[]{:S(2)}) copy-start(f32[64,6]{0,1:T(8,128)S(1)} %log_add_fusion) | copy-start | bytes 4612
  111.9 37.9 %collective-permute-start.2 = (bf16[1,1536]{1,0:T(2,128)(2,1)S(1)}, bf16[1,1536]{1,0:T(2,128)(2,1)}, u32[]{:S(2)}, u32[]{:S(2)}) collective-permute-start(bf16[1,1536]{1,0:T(2,128)(2,1)S(1)} %bitcast.170), channel_id=1, source_target_pairs={{0,4},{4,8},{8,12},{1,5},{5,9},{9,13},{2,6},{6,10},{10,14},{3,7},{... | collective-permute-start | bytes 9224 | tf_op jit(solution)/shard_map/ppermute | solution.py:16
  116.8 33.1 %collective-permute-start.3 = (bf16[1,1536]{1,0:T(2,128)(2,1)}, bf16[1,1536]{1,0:T(2,128)(2,1)}, u32[]{:S(2)}, u32[]{:S(2)}) collective-permute-start(bf16[1,1536]{1,0:T(2,128)(2,1)} %bitcast.43), channel_id=1, source_target_pairs={{4,0},{8,4},{12,8},{5,1},{9,5},{13,9},{6,2},{10,6},{14,10},{7,3},{... | collective-permute-start | bytes 9224 | tf_op jit(solution)/shard_map/ppermute | solution.py:17
  160.7 29.2 %copy-start.7 = (f32[64,6]{0,1:T(8,128)S(1)}, f32[64,6]{0,1:T(8,128)}, u32[]{:S(2)}) copy-start(f32[64,6]{0,1:T(8,128)} %copy-done.6) | copy-start | bytes 4612
  164.2 82.7 %all-reduce.11.cloned.1.call-start = ((), (), s32[]{:S(2)}) async-start(), calls=%async_computation.3 | async-start | bytes 393216 | tf_op jit(solution)/shard_map/psum | solution.py:23
Sparse Core Ops, SparseCore 0:
  52.5 18.4 all-reduce.4
  89.8 18.2 all-reduce.6
  164.4 19.4 all-reduce.8
  229.0 17.8 all-reduce.10
where the time goes:
time: 256 us; the launch traced here: 255 us
  blocking collectives  93.9 us (37%)
  waiting for transfers between devices  77 us (30%)
  matrix products  28.3 us (11%)
  local copies, waits for them, and re-layouts  18.3 us (7%)
  between operations  14.2 us (6%)
  other arithmetic  12.9 us (5%)
  starting transfers between devices  10.6 us (4%)
    psum x4, waiting for transfers between devices, pair_sum(): return lax.psum(values, 'mp')  72.7 us
    all_gather x1, blocking collectives, body(): outgrad_piece = lax.all_gather(attn_grad, 'ctx', axis=0, tiled=True)  17.8 us
    all_gather x1, blocking collectives, body(): key_piece = lax.all_gather(key_rows, 'ctx', axis=0, tiled=True)  17.3 us
    all_gather x1, blocking collectives, body(): value_piece = lax.all_gather(value_rows, 'ctx', axis=0, tiled=True)  16.3 us
    all_gather x1, blocking collectives, body(): query_piece = lax.all_gather(queries, 'ctx', axis=0, tiled=True)  15.7 us
    all_gather x1, blocking collectives, body(): lax.all_gather(row_dots, 'ctx', axis=0, tiled=True)  13.4 us
    all_gather x1, blocking collectives, body(): lax.all_gather(log_norm, 'ctx', axis=0, tiled=True)  13.4 us
    ppermute x2, starting transfers between devices, with_halo(): before = lax.ppermute(last, axis, up)  7.88 us
  transfers between devices with their start and end apart: 8, of which 5 were waited for; matrix products, arithmetic and copies ran while one was open for 2% of the time, Pallas kernels for 0%

commit v1 on v0

--- a/solution.py
+++ b/solution.py
@@ -2,6 +2,7 @@
 import jax.numpy as jnp
 from jax import lax
 from jax.sharding import PartitionSpec as P
+from jax.lax import all_gather
 
 HEAD_DIM = 64
 
@@ -20,7 +21,7 @@
 
 
 def pair_sum(values):
-    return lax.psum(values, "mp")
+    return jnp.sum(all_gather(values, axis_name="mp"), axis=0)
 
 
 def edges(values):

time: 256 us -> 167 us (0.65)
  waiting for transfers between devices: 77 us -> 0.61 us
  between operations: 14.2 us -> 1.2 us
  blocking collectives: 93.9 us -> 103 us
  matrix products: 28.3 us -> 24.3 us
    psum x4 -> x0, waiting for transfers between devices: 72.7 us -> none  [pair_sum(): return lax.psum(values, 'mp')]
    all_gather x0 -> x4, blocking collectives: none -> 8.58 us  [pair_sum(): return jnp.sum(all_gather(values, axis_name='mp'), axis=0)]
    ppermute x2, waiting for transfers between devices: 4.16 us -> 0.6 us  [with_halo(): after = lax.ppermute(initial, axis, down)]
  transfers between devices with their start and end apart: 8 -> 4, of which waited for: 5 -> 1; matrix products, arithmetic and copies ran while one was open for 2% -> 3% of each run, Pallas kernels for 0% -> 0%
where the time goes in v1:
time: 167 us; the launch traced here: 166 us
  blocking collectives  103 us (62%)
  matrix products  24.3 us (15%)
  local copies, waits for them, and re-layouts  16.9 us (10%)
  other arithmetic  10.9 us (7%)
  starting transfers between devices  9.19 us (6%)
    all_gather x1, blocking collectives, body(): outgrad_piece = lax.all_gather(attn_grad, 'ctx', axis=0, tiled=True)  18.3 us
    all_gather x1, blocking collectives, body(): key_piece = lax.all_gather(key_rows, 'ctx', axis=0, tiled=True)  17.3 us
    all_gather x1, blocking collectives, body(): value_piece = lax.all_gather(value_rows, 'ctx', axis=0, tiled=True)  16.3 us
    all_gather x1, blocking collectives, body(): query_piece = lax.all_gather(queries, 'ctx', axis=0, tiled=True)  15.7 us
    all_gather x1, blocking collectives, body(): lax.all_gather(log_norm, 'ctx', axis=0, tiled=True)  13.4 us
    all_gather x1, blocking collectives, body(): lax.all_gather(row_dots, 'ctx', axis=0, tiled=True)  13.1 us
    all_gather x4, blocking collectives, pair_sum(): return jnp.sum(all_gather(values, axis_name='mp'), axis=0)  8.58 us
    ppermute x2, starting transfers between devices, with_halo(): before = lax.ppermute(last, axis, up)  6.61 us
  transfers between devices with their start and end apart: 4, of which 1 were waited for; matrix products, arithmetic and copies ran while one was open for 3% of the time, Pallas kernels for 0%

profile of v1, /device:TPU:0, one launch (start us, length us, event | category | flops | bytes accessed | tf_op | source)
XLA Modules:
  0.0 165.9 jit_solution(6742160512597225645)
XLA Ops:
  0.7 2.6 %copy.42 = bf16[768,3,384]{0,2,1:T(8,128)(2,1)S(1)} copy(bf16[768,3,384]{2,0,1:T(8,128)(2,1)} %param.10) | data formatting | bytes 3538944 | tf_op args[3]
  5.7 17.3 %all-gather.1 = bf16[256,1,6,64]{3,2,1,0:T(8,128)(2,1)S(1)} all-gather(bf16[64,1,6,64]{3,2,1,0:T(8,128)(2,1)S(1)} %get-tuple-element.11), channel_id=3, replica_groups=mesh['groups'=2,'ctx'=4,'dp'=2,'mp'=2] {'ctx'}, dimensions={0}, use_global_device_ids=true | all-gather | bytes 245760 | tf_op jit(solution)/shard_map/all_gather | solution.py:57
  26.1 16.3 %all-gather = bf16[256,1,6,64]{3,2,1,0:T(8,128)(2,1)S(1)} all-gather(bf16[64,1,6,64]{3,2,1,0:T(8,128)(2,1)S(1)} %get-tuple-element.9), channel_id=2, replica_groups=mesh['groups'=2,'ctx'=4,'dp'=2,'mp'=2] {'ctx'}, dimensions={0}, use_global_device_ids=true | all-gather | bytes 245760 | tf_op jit(solution)/shard_map/all_gather | solution.py:58
  45.1 2.1 %all-gather.2 = f32[128,768]{1,0:T(8,128)S(1)} all-gather(f32[64,768]{1,0:T(8,128)S(1)} %fusion.103), channel_id=4, replica_groups=mesh['groups'=2,'ctx'=4,'dp'=2,'mp'=2] {'mp'}, dimensions={0}, use_global_device_ids=true | all-gather | bytes 589824 | tf_op jit(solution)/shard_map/all_gather | solution.py:24
  48.2 2.7 %collective-permute-start = (bf16[1,768]{1,0:T(2,128)(2,1)S(1)}, bf16[1,768]{1,0:T(2,128)(2,1)S(1)}, u32[]{:S(2)}, u32[]{:S(2)}) collective-permute-start(bf16[1,768]{1,0:T(2,128)(2,1)S(1)} %get-tuple-element.17), channel_id=1, source_target_pairs={{0,4},{4,8},{8,12},{1,5},{5,9},{9,13},{2,6},{6,10},{10,14},{3,7},{... | collective-permute-start | bytes 4616 | tf_op jit(solution)/shard_map/ppermute | solution.py:17
  52.2 15.7 %all-gather.5 = bf16[256,1,6,64]{3,0,2,1:T(8,128)(2,1)S(1)} all-gather(bf16[64,1,6,64]{3,0,2,1:T(8,128)(2,1)S(1)} %copy.64), channel_id=7, replica_groups=mesh['groups'=2,'ctx'=4,'dp'=2,'mp'=2] {'ctx'}, dimensions={0}, use_global_device_ids=true | all-gather | bytes 245760 | tf_op jit(solution)/shard_map/all_gather | solution.py:138
  69.0 13.4 %all-gather.7 = f32[4,64,6]{1,2,0:T(8,128)S(1)} all-gather(f32[1,64,6]{1,2,0:T(8,128)S(1)} %bitcast.176), channel_id=1, replica_groups=mesh['groups'=2,'ctx'=4,'dp'=2,'mp'=2] {'ctx'}, dimensions={0}, use_global_device_ids=true | all-gather | bytes 7680 | tf_op jit(solution)/shard_map/all_gather | solution.py:135
  83.8 1.3 fusion.19
  86.4 1.3 fusion.85
  90.2 2.2 %all-gather.3 = f32[512,256]{1,0:T(8,128)S(1)} all-gather(f32[256,256]{1,0:T(8,128)S(1)} %fusion.67), channel_id=5, replica_groups=mesh['groups'=2,'ctx'=4,'dp'=2,'mp'=2] {'mp'}, dimensions={0}, use_global_device_ids=true | all-gather | bytes 786432 | tf_op jit(solution)/shard_map/all_gather | solution.py:24
  92.7 1.6 fusion.45
  94.3 3.9 %collective-permute-start.2 = (bf16[1,1536]{1,0:T(2,128)(2,1)S(1)}, bf16[1,1536]{1,0:T(2,128)(2,1)S(1)}, u32[]{:S(2)}, u32[]{:S(2)}) collective-permute-start(bf16[1,1536]{1,0:T(2,128)(2,1)S(1)} %bitcast.178), channel_id=1, source_target_pairs={{0,4},{4,8},{8,12},{1,5},{5,9},{9,13},{2,6},{6,10},{10,14},{3,7},{... | collective-permute-start | bytes 9224 | tf_op jit(solution)/shard_map/ppermute | solution.py:17
  101.4 1.8 %reduce_sum.107 = bf16[64,384]{1,0:T(8,128)(2,1)} reduce(bf16[64,4,384]{2,1,0:T(4,128)(2,1)} %slice.107, bf16[]{:T(256)} %constant.15.clone.1), dimensions={1}, to_apply=%region_7.8 | reduce | flops 73728 | bytes 245762 | tf_op jit(solution)/shard_map/reduce_sum | solution.py:110
  103.8 1.7 %pad_maximum_fusion.2 = bf16[66,1536]{1,0:T(8,128)(2,1)} fusion(bf16[1,1536]{1,0:T(2,128)(2,1)S(1)} %collective-permute-done.3, bf16[64,1536]{1,0:T(8,128)(2,1)} %reshape.101, bf16[1,1536]{1,0:T(2,128)(2,1)S(1)} %collective-permute-done.2), kind=kLoop, calls=%fused_computation.77 | loop fusion | flops 608256 | bytes 405504 | tf_op jit(solution)/shard_map/concatenate | solution.py:19
  109.2 2.1 %fusion.27 = f32[64,768]{1,0:T(8,128)} fusion(bf16[64,384]{1,0:T(8,128)(2,1)} %reduce.1, bf16[4,768,384]{2,1,0:T(8,128)(2,1)} %param.12), kind=kOutput, calls=%fused_computation.40 | convolution fusion | flops 37748736 | bytes 835584 | tf_op jit(solution)/shard_map/dot_general | solution.py:111
  113.5 1.4 convolution_add_fusion.2
  114.9 1.4 convolution_add_fusion.1
  116.4 1.4 convolution_add_fusion
  117.8 2.2 %all-gather.4 = f32[128,768]{1,0:T(8,128)} all-gather(f32[64,768]{1,0:T(8,128)S(1)} %convolution_add_fusion), channel_id=6, replica_groups=mesh['groups'=2,'ctx'=4,'dp'=2,'mp'=2] {'mp'}, dimensions={0}, use_global_device_ids=true | all-gather | bytes 589824 | tf_op jit(solution)/shard_map/all_gather | solution.py:24
  123.7 2.3 %fusion.16 = bf16[64,1,6,64]{0,3,2,1:T(8,128)(2,1)} fusion(bf16[64,6,64]{0,2,1:T(8,128)(2,1)S(1)} %bitcast.174, f32[64,6,256]{2,0,1:T(8,128)} %copy-done.1, bf16[256,1,6,64]{0,3,2,1:T(8,128)(2,1)} %copy.48, bf16[256,1,6,64]{0,3,2,1:T(8,128)(2,1)} %copy.45, f32[64,6]{0,1:T(8,128)S(1)} %multiply_reduce_fusion, f32[64,6]{0,1:T(8,128)S(1)} %log_add_fusion, ...), kind=kOutput, calls=%fused_computation.28 | convolution fusion | flops 25706496 | bytes 888064 | tf_op jit(solution)/shard_map/qhk,khd->qhd/dot_general | solution.py:129
  126.0 13.1 %all-gather.8 = f32[4,64,6]{1,2,0:T(8,128)S(1)} all-gather(f32[1,64,6]{1,2,0:T(8,128)S(1)} %bitcast.177), channel_id=1, replica_groups=mesh['groups'=2,'ctx'=4,'dp'=2,'mp'=2] {'ctx'}, dimensions={0}, use_global_device_ids=true | all-gather | bytes 7680 | tf_op jit(solution)/shard_map/all_gather | solution.py:136
  139.2 18.3 %all_gather.54 = bf16[256,6,64]{2,1,0:T(8,128)(2,1)} all-gather(bf16[64,6,64]{2,1,0:T(8,128)(2,1)} %copy.55), channel_id=1, replica_groups=mesh['groups'=2,'ctx'=4,'dp'=2,'mp'=2] {'ctx'}, dimensions={0}, use_global_device_ids=true | all-gather | bytes 245760 | tf_op jit(solution)/shard_map/all_gather | solution.py:139
  159.7 1.9 %fusion.15 = bf16[64,1,6,64]{0,3,2,1:T(8,128)(2,1)} fusion(f32[256,6,64]{0,2,1:T(8,128)S(1)} %fusion.8, bf16[256,6,64]{0,2,1:T(8,128)(2,1)S(1)} %copy.59, bf16[256,1,6,64]{3,0,2,1:T(8,128)(2,1)S(1)} %all-gather.5, f32[256,6]{0,1:T(8,128)S(1)} %reshape.121, bf16[64,1,6,64]{3,2,1,0:T(8,128)(2,1)} %copy-done.2), kind=kOutput, calls=%fused_computation.27 | convolution fusion | flops 25509888 | bytes 890880 | tf_op jit(solution)/shard_map/qhk,qhd->khd/dot_general | solution.py:150
  163.1 2.1 %all-gather.6 = f32[128,768]{1,0:T(8,128)S(1)} all-gather(f32[64,768]{1,0:T(8,128)S(1)} %fusion.104), channel_id=8, replica_groups=mesh['groups'=2,'ctx'=4,'dp'=2,'mp'=2] {'mp'}, dimensions={0}, use_global_device_ids=true | all-gather | bytes 589824 | tf_op jit(solution)/shard_map/all_gather | solution.py:24
  (82 shorter events, 34.5 us)
Async XLA Ops:
  0.0 44.9 %copy-start = (bf16[384,768]{1,0:T(8,128)(2,1)S(1)}, bf16[384,768]{1,0:T(8,128)(2,1)}, u32[]{:S(2)}) copy-start(bf16[384,768]{1,0:T(8,128)(2,1)} %param.11) | copy-start | bytes 1769476
  0.0 3.4 %copy-start.5 = (bf16[1,64,768]{2,1,0:T(8,128)(2,1)S(1)}, bf16[1,64,768]{2,1,0:T(8,128)(2,1)}, u32[]{:S(2)}) copy-start(bf16[1,64,768]{2,1,0:T(8,128)(2,1)} %param.9) | copy-start | bytes 294916
  5.0 0.7 copy-start.3
  5.0 39.8 %copy-start.2 = (bf16[64,1,6,64]{3,2,1,0:T(8,128)(2,1)}, bf16[64,1,6,64]{3,2,1,0:T(8,128)(2,1)S(1)}, u32[]{:S(2)}) copy-start(bf16[64,1,6,64]{3,2,1,0:T(8,128)(2,1)S(1)} %get-tuple-element.9) | copy-start | bytes 147460
  26.1 21.1 %copy-start.1 = (f32[64,6,256]{2,0,1:T(8,128)}, f32[64,6,256]{2,0,1:T(8,128)S(1)}, u32[]{:S(2)}) copy-start(f32[64,6,256]{2,0,1:T(8,128)S(1)} %get-tuple-element.20) | copy-start | bytes 1179652
  44.9 2.4 %copy-start.7 = (bf16[64,6,64]{0,2,1:T(8,128)(2,1)}, bf16[64,6,64]{0,2,1:T(8,128)(2,1)S(1)}, u32[]{:S(2)}) copy-start(bf16[64,6,64]{0,2,1:T(8,128)(2,1)S(1)} %fusion.12) | copy-start | bytes 147460
  48.2 34.3 %collective-permute-start = (bf16[1,768]{1,0:T(2,128)(2,1)S(1)}, bf16[1,768]{1,0:T(2,128)(2,1)S(1)}, u32[]{:S(2)}, u32[]{:S(2)}) collective-permute-start(bf16[1,768]{1,0:T(2,128)(2,1)S(1)} %get-tuple-element.17), channel_id=1, source_target_pairs={{0,4},{4,8},{8,12},{1,5},{5,9},{9,13},{2,6},{6,10},{10,14},{3,7},{... | collective-permute-start | bytes 4616 | tf_op jit(solution)/shard_map/ppermute | solution.py:17
  50.9 31.6 %collective-permute-start.1 = (bf16[1,768]{1,0:T(2,128)(2,1)S(1)}, bf16[1,768]{1,0:T(2,128)(2,1)S(1)}, u32[]{:S(2)}, u32[]{:S(2)}) collective-permute-start(bf16[1,768]{1,0:T(2,128)(2,1)S(1)} %get-tuple-element.18), channel_id=1, source_target_pairs={{4,0},{8,4},{12,8},{5,1},{9,5},{13,9},{6,2},{10,6},{14,10},{7,3},{... | collective-permute-start | bytes 4616 | tf_op jit(solution)/shard_map/ppermute | solution.py:18
  88.2 0.8 copy-start.6
  92.4 7.2 %copy-start.4 = (bf16[64,1,6,64]{3,2,1,0:T(8,128)(2,1)S(1)}, bf16[64,1,6,64]{3,2,1,0:T(8,128)(2,1)}, u32[]{:S(2)}) copy-start(bf16[64,1,6,64]{3,2,1,0:T(8,128)(2,1)} %copy-done.3) | copy-start | bytes 147460
  92.4 7.2 %copy-start.9 = (pred[64]{0:T(512)(128)(4,1)S(1)}, pred[64]{0:T(512)(128)(4,1)}, u32[]{:S(2)}) copy-start(pred[64]{0:T(512)(128)(4,1)} %multiply_compare_fusion.1) | copy-start | bytes 196
  94.3 8.9 %collective-permute-start.2 = (bf16[1,1536]{1,0:T(2,128)(2,1)S(1)}, bf16[1,1536]{1,0:T(2,128)(2,1)S(1)}, u32[]{:S(2)}, u32[]{:S(2)}) collective-permute-start(bf16[1,1536]{1,0:T(2,128)(2,1)S(1)} %bitcast.178), channel_id=1, source_target_pairs={{0,4},{4,8},{8,12},{1,5},{5,9},{9,13},{2,6},{6,10},{10,14},{3,7},{... | collective-permute-start | bytes 9224 | tf_op jit(solution)/shard_map/ppermute | solution.py:17
  98.3 5.5 %collective-permute-start.3 = (bf16[1,1536]{1,0:T(2,128)(2,1)S(1)}, bf16[1,1536]{1,0:T(2,128)(2,1)S(1)}, u32[]{:S(2)}, u32[]{:S(2)}) collective-permute-start(bf16[1,1536]{1,0:T(2,128)(2,1)S(1)} %bitcast.179), channel_id=1, source_target_pairs={{4,0},{8,4},{12,8},{5,1},{9,5},{13,9},{6,2},{10,6},{14,10},{7,3},{... | collective-permute-start | bytes 9224 | tf_op jit(solution)/shard_map/ppermute | solution.py:18
  114.9 8.0 %copy-start.8 = (bf16[64,6,64]{0,2,1:T(8,128)(2,1)S(1)}, bf16[64,6,64]{0,2,1:T(8,128)(2,1)}, u32[]{:S(2)}) copy-start(bf16[64,6,64]{0,2,1:T(8,128)(2,1)} %copy-done.7) | copy-start | bytes 147460
